TPU v7x, 256 devices: a whole 4x4x8 slice. The times are simulated.
256 devices in a mesh: dom: 32 (over x, z_lo, y), tile: 8 (over z_hi, core).
Axes of the slice: x: 4, y: 4, z: 8 (z_hi: 4, z_lo: 2; z = z_hi * 2 + z_lo), core: 2. Of those that a mesh axis runs over, the one named last changes fastest.
Arguments:
- cotangent: bfloat16 [25, 64, 655360], P(None, None, ('dom', 'tile')), may hold values from -0.59765625 to 0.59765625
- probe_pos: float32 [3, 655360], P(None, ('dom', 'tile')), may hold values from 0 to 160, as said below
- atom_pos: float32 [3, 32768], P(None, ('dom', 'tile')), may hold values from 0 to 160, as said below
- pair_tile: int32 [15360], P(('dom', 'tile')), may hold values from 0 to 19, as said below
- pair_block: int32 [15360], P(('dom', 'tile')), may hold values from 0 to 9, as said below
- pair_count: int32 [256], P(('dom', 'tile')), may hold values from 30 to 60, as said below
- send_left: int32 [32, 1], P('dom'), may hold values from 0 to 7, as said below
- send_right: int32 [32, 1], P('dom'), may hold values from 0 to 7, as said below
Outputs:
- atom_grad: bfloat16 [25, 64, 32768], P(None, None, ('dom', 'tile'))
Inputs may be any that keep to these rules, and one draw needn't show every extreme that they name: `atom_pos`: atoms of slab s have x in [5 s, 5 s + 5]; those of its owned block b have y in [8 b, 8 b + 8]; z lies in [0, 32]. `probe_pos`: probes of device (s, t) have x in [5 s, 5 s + 5]; its local tile j, with k = j * 8 + t, has y in [8 * 8 * k / K, 8 * 8 * (k + 1) / K] where K = 160; z lies in [0, 32]. `pair_tile`: on each device the 60 slots hold distinct pairs of tile and block; each pairs a tile with a block whose y cell lies within two cells of the tile's. `pair_block`: on each device the 60 slots hold distinct pairs of tile and block. `pair_count`: some device uses all 60 slots. `send_left`: distinct within a slab's row. `send_right`: distinct within a slab's row.
All inputs are finite; a program needn't handle non-finite values.
Results may differ from a plain program's by a relative error of at most 0.0049.
Values sent between devices are 32-bit elements; how exact they have to be, the bound alone decides.
No kernel may reach another device: no remote copies, remote signals or barrier semaphores. Data moves between devices by JAX's collectives and lax.ppermute only.
A program may use at most 128 MiB of HBM per device.

v0:
```python
import jax
import jax.numpy as jnp
from jax import lax
from jax.sharding import PartitionSpec as P

cutoff = 4.0
slab_width = 5.0
block_rows = 128
group_size = 4


def extended_2(shard, sides, width):
    for axis, dim in sides:
        devices, length = (lax.axis_size(axis), shard.shape[dim])
        up = [(i, (i + 1) % devices) for i in range(devices)]
        down = [(j, i) for i, j in up]
        last = lax.slice_in_dim(shard, length - width, length, axis=dim)
        first = lax.slice_in_dim(shard, 0, width, axis=dim)
        before = lax.ppermute(last, axis, up)
        after = lax.ppermute(first, axis, down)
        shard = jnp.concatenate([before, shard, after], axis=dim)
    return shard


def harmonics(x, y, z):
    xx = x * x
    yy = y * y
    zz = z * z
    rr = xx + yy + zz
    rows = [
        jnp.ones_like(x),
        2.0 * x,
        2.0 * y,
        2.0 * z,
        3.0 * x * y,
        3.0 * y * z,
        1.5 * (3.0 * zz - rr),
        3.0 * x * z,
        1.5 * (xx - yy),
        5.0 * y * (3.0 * xx - yy),
        10.0 * x * y * z,
        5.0 * y * (5.0 * zz - rr),
        5.0 * z * (5.0 * zz - 3.0 * rr),
        5.0 * x * (5.0 * zz - rr),
        5.0 * z * (xx - yy),
        5.0 * x * (xx - 3.0 * yy),
        8.0 * x * y * (xx - yy),
        8.0 * y * z * (3.0 * xx - yy),
        8.0 * x * y * (7.0 * zz - rr),
        8.0 * y * z * (7.0 * zz - 3.0 * rr),
        35.0 * zz * zz - 30.0 * zz * rr + 3.0 * rr * rr,
        8.0 * x * z * (7.0 * zz - 3.0 * rr),
        4.0 * (xx - yy) * (7.0 * zz - rr),
        8.0 * x * z * (xx - 3.0 * yy),
        2.0 * (xx * xx - 6.0 * xx * yy + yy * yy),
    ]
    return jnp.stack(rows)


def geometry(probe, atom):
    delta = (probe[:, :, None] - atom[:, None, :]) / cutoff
    sq = delta[0] * delta[0] + delta[1] * delta[1] + delta[2] * delta[2]
    envelope = jnp.where(sq < 1.0, (1.0 - sq) * (1.0 - sq), 0.0)
    return (envelope[None] * harmonics(delta[0], delta[1], delta[2])).astype(jnp.bfloat16)


def lend_into(hot, returned, owned_blocks):
    harm, chan = (returned.shape[0], returned.shape[1])
    shaped = returned.reshape(harm, chan, hot.shape[0], block_rows)
    spread = jnp.einsum("gb,mcgi->mcbi", hot, shaped, precision=lax.Precision.HIGHEST)
    return spread.reshape(harm, chan, owned_blocks * block_rows)


def on_device(
    cotangent, probe_pos, atom_pos, pair_tile, pair_block, pair_count, send_left, send_right
):
    ndom = lax.axis_size("dom")
    ntile = lax.axis_size("tile")
    here = lax.axis_index("dom")
    own_pos = lax.all_gather(atom_pos, "tile", axis=1, tiled=True)
    owned_blocks = own_pos.shape[1] // block_rows
    ghosts = send_left.shape[1]
    edge = ghosts * block_rows
    owned_ids = jnp.arange(owned_blocks, dtype=jnp.int32)
    left_hot = (send_left[0][:, None] == owned_ids[None, :]).astype(jnp.float32)
    right_hot = (send_right[0][:, None] == owned_ids[None, :]).astype(jnp.float32)
    shaped_pos = own_pos.reshape(3, owned_blocks, block_rows)
    out_left = jnp.einsum("gb,kbi->kgi", left_hot, shaped_pos, precision=lax.Precision.HIGHEST)
    out_right = jnp.einsum("gb,kbi->kgi", right_hot, shaped_pos, precision=lax.Precision.HIGHEST)
    outgoing = jnp.concatenate([out_left, out_right], axis=1).reshape(3, 2 * edge)
    extended = extended_2(outgoing, (("dom", 1),), edge)
    box = ndom * slab_width
    left_ghost = extended[:, :edge]
    right_ghost = extended[:, extended.shape[1] - edge :]
    left_ghost = left_ghost.at[0].add(jnp.where(here == 0, -box, 0.0))
    right_ghost = right_ghost.at[0].add(jnp.where(here == ndom - 1, box, 0.0))
    table_pos = jnp.concatenate([own_pos, left_ghost, right_ghost], axis=1)
    harm, chan = (cotangent.shape[0], cotangent.shape[1])
    slots = pair_tile.shape[0]
    count = pair_count[0]

    def one_group(step, table):
        for inner in range(group_size):
            slot = step * group_size + inner
            valid = slot < count
            safe = jnp.minimum(slot, slots - 1)
            tile = pair_tile[safe]
            block = pair_block[safe]
            probe = lax.dynamic_slice_in_dim(probe_pos, tile * block_rows, block_rows, 1)
            atom = lax.dynamic_slice_in_dim(table_pos, block * block_rows, block_rows, 1)
            geom = geometry(probe, atom)
            piece = lax.dynamic_slice_in_dim(cotangent, tile * block_rows, block_rows, 2)
            term = jnp.einsum("mcp,mpa->mca", piece, geom, preferred_element_type=jnp.float32)
            old = lax.dynamic_slice_in_dim(table, block * block_rows, block_rows, 2)
            fresh = jnp.where(valid, old + term, old)
            table = lax.dynamic_update_slice_in_dim(table, fresh, block * block_rows, 2)
        return table

    start = jnp.zeros((harm, chan, table_pos.shape[1]), jnp.float32)
    table = lax.fori_loop(0, (count + group_size - 1) // group_size, one_group, start)
    span = owned_blocks * block_rows
    owned = table[:, :, :span]
    lent = table[:, :, span:]
    lent_total = lax.psum(lent, "tile")
    back = extended_2(lent_total, (("dom", 2),), edge)
    from_left = back[:, :, :edge]
    from_right = back[:, :, back.shape[2] - edge :]
    added = lend_into(left_hot, from_left, owned_blocks) + lend_into(
        right_hot, from_right, owned_blocks
    )
    mine = lax.psum_scatter(owned, "tile", scatter_dimension=2, tiled=True)
    share = span // ntile
    result = mine + lax.dynamic_slice_in_dim(added, lax.axis_index("tile") * share, share, 2)
    return result.astype(jnp.bfloat16)


def solution(mesh):
    placed = (
        P(None, None, ("dom", "tile")),
        P(None, ("dom", "tile")),
        P(None, ("dom", "tile")),
        P(("dom", "tile")),
        P(("dom", "tile")),
        P(("dom", "tile")),
        P("dom", None),
        P("dom", None),
    )
    return jax.shard_map(
        on_device,
        mesh=mesh,
        in_specs=placed,
        out_specs=P(None, None, ("dom", "tile")),
        check_vma=False,
    )
```

profile of v0, /device:TPU:1, one launch (start us, length us, event | category | flops | bytes accessed | tf_op | source)
XLA Modules:
  0.0 566.4 jit_solution(4562996639643901027)
XLA Ops:
  6.5 19.6 %all_gather.3 = f32[3,1024]{1,0:T(4,128)S(1)} all-gather(f32[3,128]{1,0:T(4,128)} %param.16), channel_id=1, replica_groups=mesh['dom'=32,'tile'=8] {'tile'}, dimensions={1}, use_global_device_ids=true | all-gather | bytes 13824 | tf_op jit(solution)/shard_map/all_gather | solution.py:80
  27.8 5.5 collective-permute-start.1
  34.0 5.9 %collective-permute-done = f32[3,128]{1,0:T(4,128)S(1)} collective-permute-done((f32[3,128]{1,0:T(4,128)S(1)}, f32[3,128]{1,0:T(4,128)S(1)}, u32[]{:S(2)}, u32[]{:S(2)}) %collective-permute-start) | collective-permute-done | bytes 1568 | tf_op jit(solution)/shard_map/ppermute | solution.py:19
  39.9 4.1 broadcast_in_dim.9
  44.0 186.0 %while.12 = (s32[]{:T(128)}, f32[25,64,1280]{2,1,0:T(8,128)}, s32[]{:T(128)}, s32[]{:T(128)}, s32[60]{0:T(128)S(1)}, /*index=5*/s32[60]{0:T(128)S(1)}, bf16[25,6...) while((s32[]{:T(128)}, f32[25,64,1280]{2,1,0:T(8,128)}, ...), condition=%wide.region_1.2_spmd, body=%wide.region_0.1_spmd.sunk | while | flops 222822464 | bytes 38376400 | solution.py:120
  47.2 0.7 fusion.61
  50.4 0.8 constant_dynamic-slice_fusion.9
  52.5 2.6 fusion.62
  56.5 2.7 fusion.63
  60.6 2.6 fusion.64
  64.6 2.6 fusion.65
  70.5 0.7 fusion.61
  73.7 0.8 constant_dynamic-slice_fusion.9
  75.8 2.7 fusion.62
  79.8 2.7 fusion.63
  83.9 2.6 fusion.64
  87.9 2.6 fusion.65
  93.7 0.7 fusion.61
  96.9 0.8 constant_dynamic-slice_fusion.9
  99.1 2.7 fusion.62
  103.1 2.7 fusion.63
  107.2 2.6 fusion.64
  111.2 2.7 fusion.65
  117.0 0.7 fusion.61
  120.2 0.8 constant_dynamic-slice_fusion.9
  122.4 2.6 fusion.62
  126.4 2.6 fusion.63
  130.3 2.6 fusion.64
  134.2 2.7 fusion.65
  140.1 0.7 fusion.61
  143.3 0.8 constant_dynamic-slice_fusion.9
  145.5 2.7 fusion.62
  149.5 2.8 fusion.63
  153.7 2.7 fusion.64
  157.8 2.6 fusion.65
  163.6 0.7 fusion.61
  166.8 0.8 constant_dynamic-slice_fusion.9
  169.0 2.6 fusion.62
  172.9 2.6 fusion.63
  176.9 2.6 fusion.64
  180.9 2.8 fusion.65
  186.9 0.7 fusion.61
  190.1 0.8 constant_dynamic-slice_fusion.9
  192.2 2.7 fusion.62
  196.2 2.6 fusion.63
  200.2 2.8 fusion.64
  204.3 2.6 fusion.65
  210.1 0.7 fusion.61
  213.3 0.8 constant_dynamic-slice_fusion.9
  215.4 2.6 fusion.62
  219.4 2.6 fusion.63
  223.4 2.6 fusion.64
  227.4 2.6 fusion.65
  230.0 2.8 slice.117
  232.9 6.8 %slice.116 = f32[25,64,1024]{2,1,0:T(8,128)} slice(f32[25,64,1280]{2,1,0:T(8,128)} %get-tuple-element.77), slice={[0:25], [0:64], [0:1024]} | slice | bytes 13107200 | tf_op jit(solution)/shard_map/slice | solution.py:122
  239.8 228.2 %all-reduce.2.cloned.1.call-done = f32[25,64,256]{2,1,0:T(8,128)} async-done(((f32[25,64,256]{2,1,0:T(8,128)}), f32[25,64,256]{2,1,0:T(8,128)}) %all-reduce.2.cloned.1.call-update) | async-done | bytes 1638416 | tf_op jit(solution)/shard_map/psum | solution.py:124
  468.0 1.5 fusion.44
  469.5 5.1 collective-permute-start.3
  474.6 26.5 %collective-permute-done.3 = f32[25,64,128]{2,1,0:T(8,128)S(1)} collective-permute-done((f32[25,64,128]{2,1,0:T(8,128)S(1)}, f32[25,64,128]{2,1,0:T(8,128)S(1)}, u32[]{:S(2)}, u32[]{:S(2)}) %collective-permute-start.3) | collective-permute-done | bytes 819232 | tf_op jit(solution)/shard_map/ppermute | solution.py:20
  501.1 6.6 %collective-permute-done.2 = f32[25,64,128]{2,1,0:T(8,128)S(1)} collective-permute-done((f32[25,64,128]{2,1,0:T(8,128)S(1)}, f32[25,64,128]{2,1,0:T(8,128)S(1)}, u32[]{:S(2)}, u32[]{:S(2)}) %collective-permute-start.2) | collective-permute-done | bytes 819232 | tf_op jit(solution)/shard_map/ppermute | solution.py:19
  507.7 3.3 add_bitcast_fusion
  511.0 7.7 %add.262 = f32[25,64,1024]{2,1,0:T(8,128)} reshape(f32[25,64,8,128]{3,2,1,0:T(8,128)} %add_bitcast_fusion) | data formatting | bytes 13107200 | tf_op jit(solution)/shard_map/add | solution.py:128
  518.7 38.6 %reduce-scatter.2.cloned.1.call-done = f32[25,64,128]{2,1,0:T(8,128)} async-done(((f32[25,64,1024]{2,1,0:T(8,128)}), f32[25,64,128]{2,1,0:T(8,128)}) %reduce-scatter.2.cloned.1.call-update) | async-done | bytes 819216 | tf_op jit(solution)/shard_map/reduce_scatter | solution.py:131
  557.3 2.3 add_convert_fusion
  (862 shorter events, 22.5 us)
Async XLA Ops:
  6.5 461.5 %all-reduce.2.cloned.1.call-start = ((), (), s32[]{:S(2)}) async-start(), calls=%async_computation.2 | async-start | bytes 3276800 | tf_op jit(solution)/shard_map/psum | solution.py:124
  27.8 6.2 %collective-permute-start.1 = (f32[3,128]{1,0:T(4,128)S(1)}, f32[3,128]{1,0:T(4,128)S(1)}, u32[]{:S(2)}, u32[]{:S(2)}) collective-permute-start(f32[3,128]{1,0:T(4,128)S(1)} %get-tuple-element.139), channel_id=1, source_target_pairs={{8,0},{16,8},{24,16},{32,24},{40,32},{48,40},{56,48},{64,56},{72,6... | collective-permute-start | bytes 4616 | tf_op jit(solution)/shard_map/ppermute | solution.py:20
  33.2 6.7 %collective-permute-start = (f32[3,128]{1,0:T(4,128)S(1)}, f32[3,128]{1,0:T(4,128)S(1)}, u32[]{:S(2)}, u32[]{:S(2)}) collective-permute-start(f32[3,128]{1,0:T(4,128)S(1)} %get-tuple-element.138), channel_id=1, source_target_pairs={{0,8},{8,16},{16,24},{24,32},{32,40},{40,48},{48,56},{56,64},{64,7... | collective-permute-start | bytes 4616 | tf_op jit(solution)/shard_map/ppermute | solution.py:19
  39.9 4.1 copy-start
  39.9 4.1 copy-start.1
  232.8 324.5 %reduce-scatter.2.cloned.1.call-start = ((), (), s32[]{:S(2)}) async-start(), calls=%async_computation.1 | async-start | bytes 7372800 | tf_op jit(solution)/shard_map/reduce_scatter | solution.py:131
  469.5 31.6 %collective-permute-start.3 = (f32[25,64,128]{2,1,0:T(8,128)S(1)}, f32[25,64,128]{2,1,0:T(8,128)S(1)}, u32[]{:S(2)}, u32[]{:S(2)}) collective-permute-start(f32[25,64,128]{2,1,0:T(8,128)S(1)} %get-tuple-element.137), channel_id=1, source_target_pairs={{8,0},{16,8},{24,16},{32,24},{40,32},{48,40},{56,48},{64,56},{72,6... | collective-permute-start | bytes 2457608 | tf_op jit(solution)/shard_map/ppermute | solution.py:20
  474.6 33.1 %collective-permute-start.2 = (f32[25,64,128]{2,1,0:T(8,128)S(1)}, f32[25,64,128]{2,1,0:T(8,128)S(1)}, u32[]{:S(2)}, u32[]{:S(2)}) collective-permute-start(f32[25,64,128]{2,1,0:T(8,128)S(1)} %get-tuple-element.136), channel_id=1, source_target_pairs={{0,8},{8,16},{16,24},{24,32},{32,40},{40,48},{48,56},{56,64},{64,7... | collective-permute-start | bytes 2457608 | tf_op jit(solution)/shard_map/ppermute | solution.py:19
Sparse Core Ops, SparseCore 0:
  233.0 235.0 all-reduce.1
  470.6 86.6 reduce-scatter.1
where the time goes:
time: 572 us; the launch traced here: 566 us
  waiting for transfers between devices  306 us (53%)
  matrix products  85.3 us (15%)
  loops' own time  67.4 us (12%)
  local copies, waits for them, and re-layouts  40.1 us (7%)
  other arithmetic  22 us (4%)
  blocking collectives  19.6 us (3%)
  between operations  15.4 us (3%)
  starting transfers between devices  10.6 us (2%)
    psum x1, waiting for transfers between devices, on_device(): lent_total = lax.psum(lent, 'tile')  228 us
    dot_general x32, matrix products, one_group(): jnp.einsum('mcp,mpa->mca', piece, geom, preferred_element_type=jnp.float32)  85.1 us
    another operation x1, loops' own time, on_device(): lax.fori_loop(0, (count + group_size - 1) // group_size, one_group, start)  67.4 us
    reduce_scatter x1, waiting for transfers between devices, on_device(): mine = lax.psum_scatter(owned, 'tile', scatter_dimension=2, tiled=True)  38.6 us
    ppermute x2, waiting for transfers between devices, extended_2(): after = lax.ppermute(first, axis, down)  26.6 us
    all_gather x1, blocking collectives, on_device(): own_pos = lax.all_gather(atom_pos, 'tile', axis=1, tiled=True)  19.6 us
    ppermute x2, waiting for transfers between devices, extended_2(): before = lax.ppermute(last, axis, up)  12.5 us
  transfers between devices with their start and end apart: 6, of which 5 were waited for; matrix products, arithmetic and copies ran while one was open for 3% of the time, Pallas kernels for 0%

commit v1 on v0

v1 whole, which is shorter than its diff:
```python
import functools

import jax
import jax.numpy as jnp
from jax import lax
from jax.experimental import pallas as pl
from jax.experimental.pallas import tpu as pltpu
from jax.sharding import PartitionSpec as P

cutoff = 4.0
slab_width = 5.0
rows = 128
offsets = (2, 1, 3, 0)
tiles_max = 20
every = tuple(range(25))


def harmonics(e, x, y, z, xx, yy, zz, wanted):
    rr = xx + yy + zz
    ex = e * x
    ey = e * y
    ez = e * z
    exy = ex * y
    eyz = ey * z
    exz = ex * z
    d = xx - yy
    ed = e * d
    z3 = 3.0 * zz
    z5 = 5.0 * zz
    z7 = 7.0 * zz
    r3 = 3.0 * rr
    f = 3.0 * xx - yy
    k = xx - 3.0 * yy
    g = z5 - rr
    h = z5 - r3
    w = z7 - rr
    v = z7 - r3
    made = {
        0: lambda: e,
        1: lambda: 2.0 * ex,
        2: lambda: 2.0 * ey,
        3: lambda: 2.0 * ez,
        4: lambda: 3.0 * exy,
        5: lambda: 3.0 * eyz,
        6: lambda: (1.5 * e) * (z3 - rr),
        7: lambda: 3.0 * exz,
        8: lambda: 1.5 * ed,
        9: lambda: (5.0 * ey) * f,
        10: lambda: 10.0 * (exy * z),
        11: lambda: (5.0 * ey) * g,
        12: lambda: (5.0 * ez) * h,
        13: lambda: (5.0 * ex) * g,
        14: lambda: (5.0 * ez) * d,
        15: lambda: (5.0 * ex) * k,
        16: lambda: (8.0 * exy) * d,
        17: lambda: (8.0 * eyz) * f,
        18: lambda: (8.0 * exy) * w,
        19: lambda: (8.0 * eyz) * v,
        20: lambda: e * (z5 * (z7 - 6.0 * rr) + r3 * rr),
        21: lambda: (8.0 * exz) * v,
        22: lambda: (4.0 * ed) * w,
        23: lambda: (8.0 * exz) * k,
        24: lambda: (2.0 * e) * (xx * k - yy * f),
    }
    return [made[m]() for m in wanted]


far = 1000.0
chunk = 16


def geometry(tile, r, atom, probe_ref):
    p = probe_ref[pl.ds(pl.multiple_of(tile * rows + r * chunk, chunk), chunk), :]
    x = p[:, 0:1] - atom[0]
    y = p[:, 1:2] - atom[1]
    z = p[:, 2:3] - atom[2]
    xx = x * x
    yy = y * y
    zz = z * z
    inside = jnp.maximum(1.0 - (xx + yy + zz), 0.0)
    return harmonics(inside * inside, x, y, z, xx, yy, zz, every)


def add_term(m, side, tiles, cot_ref, geom, top_ref, bottom_ref):
    piece = jnp.concatenate(
        [cot_ref[m, :, pl.ds(pl.multiple_of(tile * rows, rows), rows)] for tile in tiles], axis=1
    )
    term = jnp.dot(piece, geom[m], preferred_element_type=jnp.float32)
    half = term.shape[0] // 2
    at = slice(m * half, m * half + half)
    top_ref[side, at, :] = top_ref[side, at, :] + term[:half]
    bottom_ref[side, at, :] = bottom_ref[side, at, :] + term[half:]


def make_and_add(make, add, atoms, probe_ref, cot_ref, made, used, outs):
    chunks = [(n, r) for n in range(2) for r in range(rows // chunk)] if make else []
    turns = len(chunks) or 1
    for turn in range(turns):
        if make:
            n, r = chunks[turn]
            values = geometry(make[n], r, atoms[n], probe_ref)
            at = slice(n * rows + r * chunk, n * rows + r * chunk + chunk)
            for m, value in enumerate(values):
                made[m, at, :] = value.astype(jnp.bfloat16)
        if add:
            side, tiles = add
            for m in range(turn * len(every) // turns, (turn + 1) * len(every) // turns):
                add_term(m, side, tiles, cot_ref, used, *outs)


def fill_lists(slots, tile_ref, block_ref, count, lists, counts):
    def clear(b, carry):
        counts[b] = 0
        return carry

    lax.fori_loop(0, 10, clear, 0)

    def put(j, carry):
        b = block_ref[j]
        n = counts[b]
        lists[b * tiles_max + n] = tile_ref[j]
        counts[b] = n + 1
        return carry

    lax.fori_loop(0, jnp.minimum(count, slots), put, 0)


def list_steps(side, b, atom, bounds, lists, counts, steps, n):
    ymin = jnp.min(atom[1])
    ymax = jnp.max(atom[1])

    def keep(j, found):
        tile = lists[b * tiles_max + j]
        gap = jnp.maximum(ymin - bounds[1, tile], bounds[0, tile] - ymax)
        near = gap < 1.0
        at = 3 * n + 3 * (found // 2)
        odd = found % 2

        @pl.when(near)
        def _():
            steps[at] = side
            steps[at + 1 + odd] = tile

            @pl.when(odd == 0)
            def _():
                steps[at + 2] = -1

        return found + jnp.where(near, 1, 0)

    return n + (lax.fori_loop(0, counts[b], keep, 0) + 1) // 2


def kernel(kind, slots, box, meta, tile_ref, block_ref, bounds, probe_ref, pos_ref, cot_ref, after_ref, *rest):
    *outs, first_geom, second_geom, atom_ref, lists, counts, steps = rest
    step = pl.program_id(0)

    @pl.when(step == 0)
    def _():
        fill_lists(slots, tile_ref, block_ref, meta[0], lists, counts)

    core = meta[2]
    if kind == "main":
        halves = [ref.at[0] for ref in outs]
    else:
        halves = [outs[0].at[0], outs[0].at[1]]
    for ref in halves:
        ref[...] = jnp.zeros(ref.shape, jnp.float32)
    n = 0
    for side in range(2):
        if kind == "main":
            offset = jnp.where(step == 0, 2, jnp.where(step == 1, 1, jnp.where(step == 2, 3, 0)))
            chip = lax.rem(meta[1] + offset, 4)
            b = chip * 2 + (core if side == 0 else 1 - core)
            place = lax.bitwise_xor(chip, meta[1])
            atom = [pos_ref[place, side, i : i + 1, :] for i in range(3)]
        else:
            which = core if side == 0 else 1 - core
            b = 8 + which
            lent_left = jnp.max(pos_ref[0, 0, 9:10, :])
            lent_right = jnp.max(pos_ref[0, 0, 13:14, :])
            source = jnp.where(which == 0, lent_left, lent_right).astype(jnp.int32)
            place = lax.bitwise_xor(source // 2, meta[1])
            other = jnp.where(lax.rem(source, 2) == core, 0, 1)
            left = [pos_ref[place, other, 5 + i : 6 + i, :] for i in range(3)]
            right = [pos_ref[place, other, 10 + i : 11 + i, :] for i in range(3)]
            left[0] = left[0] + jnp.where(meta[3] == 0, -box, 0.0)
            right[0] = right[0] + jnp.where(meta[3] == meta[4] - 1, box, 0.0)
            atom = [jnp.where(which == 0, l, r) for l, r in zip(left, right)]
        atom = [a * 0.25 for a in atom]
        for i in range(3):
            atom_ref[side, i : i + 1, :] = atom[i]
        n = list_steps(side, b, atom, bounds, lists, counts, steps, n)

    def one(j):
        side, first, second = steps[3 * j], steps[3 * j + 1], steps[3 * j + 2]
        atom = [atom_ref[side, i : i + 1, :] for i in range(3)]
        moved = [atom[0] - jnp.where(second < 0, far, 0.0), *atom[1:]]
        return side, (first, jnp.maximum(second, 0)), (atom, moved)

    def turn(make, add, made, used):
        made_step = one(make) if make is not None else (None, None, None)
        added = one(add)[:2] if add is not None else None
        make_and_add(made_step[1], added, made_step[2], probe_ref, cot_ref, made, used, halves)

    @pl.when(n > 0)
    def _():
        turn(0, None, first_geom, None)

    def both(k, carry):
        turn(2 * k + 1, 2 * k, second_geom, first_geom)
        turn(2 * k + 2, 2 * k + 1, first_geom, second_geom)
        return carry

    whole = jnp.maximum(n - 1, 0) // 2
    lax.fori_loop(0, whole, both, 0)

    @pl.when(n - 2 * whole == 1)
    def _():
        turn(None, n - 1, None, first_geom)

    @pl.when(n - 2 * whole == 2)
    def _():
        turn(n - 1, n - 2, second_geom, first_geom)
        turn(None, n - 1, None, second_geom)


def compute(kind, meta, pair_tile, pair_block, bounds, probe, pos, cot, box, after):
    harm, chan, width = cot.shape
    height = harm * chan // 2
    slots = pair_tile.shape[0]
    smem = pl.BlockSpec(memory_space=pltpu.SMEM)
    whole = pl.BlockSpec(memory_space=pltpu.VMEM)
    any_space = pl.BlockSpec(memory_space=pl.ANY)
    if kind == "main":
        grid = 4
        shape = [jax.ShapeDtypeStruct((4, 2, height, rows), jnp.float32)] * 2
        out_specs = [
            pl.BlockSpec((1, 2, height, rows), lambda i: (jnp.where(i == 1, 2, jnp.where(i == 2, 1, i)), 0, 0, 0)),
            pl.BlockSpec((1, 2, height, rows), lambda i: (i, 0, 0, 0)),
        ]
    else:
        grid = 1
        shape = [jax.ShapeDtypeStruct((2, 2, height, rows), jnp.float32)]
        out_specs = [pl.BlockSpec((2, 2, height, rows), lambda i: (0, 0, 0, 0))]
    geom = pltpu.VMEM((harm, 2 * rows, rows), jnp.bfloat16)
    return pl.pallas_call(
        functools.partial(kernel, kind, slots, box),
        out_shape=shape,
        grid=(grid,),
        in_specs=[smem, smem, smem, smem, whole, whole, whole, any_space],
        out_specs=out_specs,
        scratch_shapes=[
            geom,
            geom,
            pltpu.VMEM((2, 8, rows), jnp.float32),
            pltpu.SMEM((10 * tiles_max,), jnp.int32),
            pltpu.SMEM((16,), jnp.int32),
            pltpu.SMEM((3 * (2 * tiles_max + 4),), jnp.int32),
        ],
        compiler_params=pltpu.CompilerParams(vmem_limit_bytes=24 * 1024 * 1024),
        cost_estimate=pl.CostEstimate(flops=0, bytes_accessed=0, transcendentals=0),
        name=kind,
    )(meta, pair_tile, pair_block, bounds, probe, pos, cot, after)


def hold_kernel(cot_hbm, probe_ref, bounds_ref, meta_ref, out_ref, token_ref, sem):
    copy = pltpu.make_async_copy(cot_hbm, out_ref, sem)
    copy.start()
    token_ref[...] = jnp.zeros_like(token_ref)
    copy.wait()


def hold(cot, probe, bounds, meta):
    any_space = pl.BlockSpec(memory_space=pl.ANY)
    whole = pl.BlockSpec(memory_space=pltpu.VMEM)
    return pl.pallas_call(
        hold_kernel,
        out_shape=[
            pltpu.VMEM(cot.shape, cot.dtype),
            jax.ShapeDtypeStruct((15, rows), jnp.float32),
        ],
        in_specs=[pl.BlockSpec(memory_space=pltpu.HBM), any_space, any_space, any_space],
        out_specs=[whole, whole],
        scratch_shapes=[pltpu.SemaphoreType.DMA],
        compiler_params=pltpu.CompilerParams(vmem_limit_bytes=16 * 1024 * 1024),
        name="hold",
    )(pltpu.with_memory_space_constraint(cot, pltpu.HBM), probe, bounds, meta)


def on_device(
    cotangent, probe_pos, atom_pos, pair_tile, pair_block, pair_count, send_left, send_right
):
    ndom = lax.axis_size("dom")
    ntile = lax.axis_size("tile")
    slab = lax.axis_index("dom")
    place = lax.axis_index("tile")
    core = place % 2
    chips = ntile // 2
    box = ndom * slab_width
    up = [(i, (i + 1) % ndom) for i in range(ndom)]
    down = [(j, i) for i, j in up]
    swap = [(i, i ^ 1) for i in range(ntile)]

    def along(o):
        return [(z * 2 + c, ((z + o) % chips) * 2 + c) for z in range(chips) for c in range(2)]

    ids = jnp.concatenate([send_left, send_right], axis=0)[:, :1].astype(jnp.float32)
    own = jnp.concatenate([atom_pos, jnp.broadcast_to(ids, (2, rows))], axis=0)
    own = lax.optimization_barrier(own)
    before = lax.ppermute(own, "dom", up)
    after = lax.ppermute(own, "dom", down)
    meta = jnp.stack([pair_count[0], place // 2, core, slab, jnp.int32(ndom)])
    shaped = (probe_pos[1] * 0.25).reshape(-1, rows)
    bounds = jnp.stack([jnp.min(shaped, axis=1), jnp.max(shaped, axis=1)])
    probe = (probe_pos * 0.25).T
    cot, token = hold(cotangent, probe, bounds, meta)
    three = jnp.concatenate([own, before, after], axis=0)
    three = three + token
    pos = three[None]
    for bit in (1, 2, 4):
        other = lax.ppermute(pos, "tile", [(i, i ^ bit) for i in range(ntile)])
        pos = jnp.concatenate([pos, other], axis=0)
    pos = pos.reshape(chips, 2, *three.shape)

    home = []
    for s in range(ndom):
        for t in range(ntile):
            way = 1 if t % 2 else -1
            home.append((s * ntile + t, ((s + way) % ndom) * ntile + t))
    lent_id = jnp.where(core == 0, send_right[0, 0], send_left[0, 0])
    owner = [(place // 2 + o) % chips * 2 for o in offsets]
    is_keep = [o + core == lent_id for o in owner]
    is_send = [o + 1 - core == lent_id for o in owner]

    args = (meta, pair_tile, pair_block, bounds, probe, pos, cot, box)
    (lent,) = compute("lent", *args, atom_pos)
    lent = lent[:, 0] + lax.ppermute(lent[:, 1], "tile", swap)
    back = lax.ppermute(lent, ("dom", "tile"), home)
    top, bottom = compute("main", *args, lent)

    def over_cores(part, half, first, blocks):
        at = slice(first, first + 2)
        second = lax.broadcasted_iota(jnp.int32, (2, 1, 1), 0) == 1
        two = jnp.where(second, is_send[blocks[1]], is_send[blocks[0]])
        send = part[at, 1] + jnp.where(two, back[half], 0.0)
        got = lax.ppermute(send, "tile", swap)
        return [
            part[first + i, 0] + jnp.where(is_keep[n], back[half], 0.0) + got[i]
            for i, n in enumerate(blocks)
        ]

    far_top, last_top = over_cores(top, 0, 0, (0, 2))
    far_bottom, next_bottom = over_cores(bottom, 1, 0, (0, 1))
    far_ahead = lax.ppermute(far_top, "tile", along(1))
    far_behind = lax.ppermute(far_bottom, "tile", along(-1))
    near_behind = lax.ppermute(last_top, "tile", along(-1))
    near_ahead = lax.ppermute(next_bottom, "tile", along(1))
    next_top, here_top = over_cores(top, 0, 2, (1, 3))
    last_bottom, here_bottom = over_cores(bottom, 1, 2, (2, 3))
    sums = lax.optimization_barrier((next_top + far_ahead, last_bottom + far_behind))
    end_ahead = lax.ppermute(sums[0], "tile", along(1))
    end_behind = lax.ppermute(sums[1], "tile", along(-1))
    halves = (here_top + near_behind + end_ahead, here_bottom + near_ahead + end_behind)
    shape = (cotangent.shape[0], -1, rows)
    total = jnp.concatenate([h.astype(jnp.bfloat16).reshape(shape) for h in halves], axis=1)
    return total


def solution(mesh):
    placed = (
        P(None, None, ("dom", "tile")),
        P(None, ("dom", "tile")),
        P(None, ("dom", "tile")),
        P(("dom", "tile")),
        P(("dom", "tile")),
        P(("dom", "tile")),
        P("dom", None),
        P("dom", None),
    )
    return jax.shard_map(
        on_device,
        mesh=mesh,
        in_specs=placed,
        out_specs=P(None, None, ("dom", "tile")),
        check_vma=False,
    )
```

time: 572 us -> 125 us (0.22)
  waiting for transfers between devices: 306 us -> 54.4 us
  matrix products: 85.3 us -> 0 us
  loops' own time: 67.4 us -> 0 us
  local copies, waits for them, and re-layouts: 40.1 us -> 4.04 us
  starting transfers between devices: 10.6 us -> 32.7 us
  blocking collectives: 19.6 us -> 0 us
  Pallas kernels: 0 us -> 17.4 us
  between operations: 15.4 us -> 2.25 us
  other arithmetic: 22 us -> 13.6 us
    psum x1 -> x0, waiting for transfers between devices: 228 us -> none  [on_device(): lent_total = lax.psum(lent, 'tile')]
    dot_general x32 -> x0, matrix products: 85.1 us -> none  [one_group(): jnp.einsum('mcp,mpa->mca', piece, geom, preferred_element_type=jnp.float32)]
    another operation x1 -> x0, loops' own time: 67.4 us -> none  [on_device(): lax.fori_loop(0, (count + group_size - 1) // group_size, one_group, start)]
    reduce_scatter x1 -> x0, waiting for transfers between devices: 38.6 us -> none  [on_device(): mine = lax.psum_scatter(owned, 'tile', scatter_dimension=2, tiled=True)]
    ppermute x4 -> x17, starting transfers between devices: 10.6 us -> 32.7 us  [the longest x3 9.31 us: on_device(): other = lax.ppermute(pos, 'tile', [(i, i ^ bit) for i in range(ntile)])]
    all_gather x1 -> x0, blocking collectives: 19.6 us -> none  [on_device(): own_pos = lax.all_gather(atom_pos, 'tile', axis=1, tiled=True)]
    pallas_call x0 -> x3, Pallas kernels: none -> 17.4 us  [the longest x2 14 us: compute(): pl.pallas_call(functools.partial(kernel, kind, slots, box), out_shape=sha...]
    dynamic_slice x24 -> x0, local copies, waits for them, and re-layouts: 16.9 us -> none  [the longest x8 6.08 us: one_group(): lax.dynamic_slice_in_dim(table_pos, block * block_rows, block_rows, 1)]
  transfers between devices with their start and end apart: 6 -> 17, of which waited for: 5 -> 13; matrix products, arithmetic and copies ran while one was open for 3% -> 7% of each run, Pallas kernels for 0% -> 12%
where the time goes in v1:
time: 125 us; the launch traced here: 124 us
  waiting for transfers between devices  54.4 us (44%)
  starting transfers between devices  32.7 us (26%)
  Pallas kernels  17.4 us (14%)
  other arithmetic  13.6 us (11%)
  local copies, waits for them, and re-layouts  4.04 us (3%)
  between operations  2.25 us (2%)
    ppermute x1, waiting for transfers between devices, on_device(): far_ahead = lax.ppermute(far_top, 'tile', along(1))  26.1 us
    pallas_call x2, Pallas kernels, compute(): pl.pallas_call(functools.partial(kernel, kind, slots, box), out_shape=sha...  14 us
    ppermute x3, starting transfers between devices, on_device(): other = lax.ppermute(pos, 'tile', [(i, i ^ bit) for i in range(ntile)])  9.31 us
    ppermute x1, waiting for transfers between devices, on_device(): near_ahead = lax.ppermute(next_bottom, 'tile', along(1))  7.54 us
    ppermute x1, waiting for transfers between devices, on_device(): end_ahead = lax.ppermute(sums[0], 'tile', along(1))  7.37 us
    ppermute x1, starting transfers between devices, on_device(): after = lax.ppermute(own, 'dom', down)  4.99 us
    ppermute x1, starting transfers between devices, on_device(): lent = lent[:, 0] + lax.ppermute(lent[:, 1], 'tile', swap)  4.25 us
    ppermute x3, waiting for transfers between devices, on_device(): other = lax.ppermute(pos, 'tile', [(i, i ^ bit) for i in range(ntile)])  4.14 us
  transfers between devices with their start and end apart: 17, of which 13 were waited for; matrix products, arithmetic and copies ran while one was open for 7% of the time, Pallas kernels for 12%

profile of v1, /device:TPU:1, one launch (start us, length us, event | category | flops | bytes accessed | tf_op | source)
XLA Modules:
  0.0 124.4 jit_solution(1991294210659776863)
XLA Ops:
  1.3 0.1 add_convert_fusion
  1.4 0.1 pad.15.clone
  1.5 0.8 pad_maximum_fusion.4
  2.2 2.1 %collective-permute-start = (f32[5,128]{1,0:T(8,128)S(1)}, f32[5,128]{1,0:T(8,128)S(1)}, u32[]{:S(2)}, u32[]{:S(2)}) collective-permute-start(f32[5,128]{1,0:T(8,128)S(1)} %pad_maximum_fusion.4), channel_id=1, source_target_pairs={{0,8},{8,16},{16,24},{24,32},{32,40},{40,48},{48,56},{56,64},{64,7... | collective-permute-start | bytes 7688 | tf_op jit(solution)/shard_map/ppermute | solution.py:310
  4.3 5.0 %collective-permute-start.1 = (f32[5,128]{1,0:T(8,128)S(1)}, f32[5,128]{1,0:T(8,128)S(1)}, u32[]{:S(2)}, u32[]{:S(2)}) collective-permute-start(f32[5,128]{1,0:T(8,128)S(1)} %pad_maximum_fusion.4), channel_id=1, source_target_pairs={{8,0},{16,8},{24,16},{32,24},{40,32},{48,40},{56,48},{64,56},{72,6... | collective-permute-start | bytes 7688 | tf_op jit(solution)/shard_map/ppermute | solution.py:311
  9.3 0.8 multiply_reduce_fusion
  10.1 0.8 broadcast_multiply_fusion
  10.9 0.1 bitcast_reduce_fusion.1
  11.7 0.4 copy.17
  12.2 0.1 stack.24.meta_ref.meta
  12.3 3.4 %hold.1 = (bf16[25,64,2560]{2,1,0:T(8,128)(2,1)S(1)}, f32[15,128]{1,0:T(8,128)S(1)}) custom-call(bf16[25,64,2560]{2,1,0:T(8,128)(2,1)} %cot_hbm.1, f32[2560,3]{1,0:T(8,128)S(1)} %bitcast.148, f32[2,20]{1,0:T(2,128)S(1)} %pad_maximum_fusion.5.bounds_ref.bounds, s32[5]{0:T(128)S(1)} %stack.24.meta_ref.meta), custom_call_target="tpu_custom_call" | custom-call | tf_op jit(solution)/shard_map/hold/pallas_call | solution.py:276
  15.6 0.0 copy-start
  15.7 0.0 collective-permute-done
  15.7 0.0 collective-permute-done.1
  15.7 2.5 %collective-permute-start.2 = (f32[1,15,128]{2,1,0:T(8,128)S(1)}, f32[1,15,128]{2,1,0:T(8,128)S(1)}, u32[]{:S(2)}, u32[]{:S(2)}) collective-permute-start(f32[1,15,128]{2,1,0:T(8,128)S(1)} %fusion.21), channel_id=1, source_target_pairs={{0,1},{1,0},{2,3},{3,2},{4,5},{5,4},{6,7},{7,6},{8,9},{9,8},{10,11... | collective-permute-start | bytes 23048 | tf_op jit(solution)/shard_map/ppermute | solution.py:321
  18.2 0.8 collective-permute-done.2
  19.0 1.6 %collective-permute-start.3 = (f32[2,15,128]{2,1,0:T(8,128)S(1)}, f32[2,15,128]{2,1,0:T(8,128)S(1)}, u32[]{:S(2)}, u32[]{:S(2)}) collective-permute-start(f32[2,15,128]{2,1,0:T(8,128)S(1)} %pad_maximum_fusion.3), channel_id=1, source_target_pairs={{0,2},{1,3},{2,0},{3,1},{4,6},{5,7},{6,4},{7,5},{8,10},{9,11},{10,... | collective-permute-start | bytes 46088 | tf_op jit(solution)/shard_map/ppermute | solution.py:321
  20.6 1.9 %collective-permute-done.3 = f32[2,15,128]{2,1,0:T(8,128)S(1)} collective-permute-done((f32[2,15,128]{2,1,0:T(8,128)S(1)}, f32[2,15,128]{2,1,0:T(8,128)S(1)}, u32[]{:S(2)}, u32[]{:S(2)}) %collective-permute-start.3) | collective-permute-done | bytes 15392 | tf_op jit(solution)/shard_map/ppermute | solution.py:321
  22.5 5.3 %collective-permute-start.4 = (f32[4,15,128]{2,1,0:T(8,128)S(1)}, f32[4,15,128]{2,1,0:T(8,128)S(1)}, u32[]{:S(2)}, u32[]{:S(2)}) collective-permute-start(f32[4,15,128]{2,1,0:T(8,128)S(1)} %pad_maximum_fusion.2), channel_id=1, source_target_pairs={{0,4},{1,5},{2,6},{3,7},{4,0},{5,1},{6,2},{7,3},{8,12},{9,13},{10,... | collective-permute-start | bytes 92168 | tf_op jit(solution)/shard_map/ppermute | solution.py:321
  27.8 1.4 %collective-permute-done.4 = f32[4,15,128]{2,1,0:T(8,128)S(1)} collective-permute-done((f32[4,15,128]{2,1,0:T(8,128)S(1)}, f32[4,15,128]{2,1,0:T(8,128)S(1)}, u32[]{:S(2)}, u32[]{:S(2)}) %collective-permute-start.4) | collective-permute-done | bytes 30752 | tf_op jit(solution)/shard_map/ppermute | solution.py:321
  29.2 0.0 copy-done.4
  29.2 0.0 copy-done.5
  29.2 0.0 copy-done.6
  29.2 2.6 %lent.1 = f32[2,2,800,128]{3,2,1,0:T(8,128)S(1)} custom-call(s32[5]{0:T(128)S(1)} %stack.24.meta_ref.meta, s32[60]{0:T(128)S(1)} %copy-done.5, s32[60]{0:T(128)S(1)} %copy-done.6, f32[2,20]{1,0:T(2,128)S(1)} %pad_maximum_fusion.5.bounds_ref.bounds, f32[2560,3]{1,0:T(8,128)S(1)} %bitcast.149, f32[4,2,15,128]{3,2,1,0:T(8,128)S(1)} %bitcast.151, ...), custom_call_target="tpu_custom_call" | custom-call | tf_op jit(solution)/shard_map/lent/pallas_call | solution.py:246
  31.8 0.0 copy-done
  31.9 0.1 slice_bitcast_fusion.4
  31.9 4.2 %collective-permute-start.5 = (f32[2,800,128]{2,1,0:T(8,128)S(1)}, f32[2,800,128]{2,1,0:T(8,128)S(1)}, u32[]{:S(2)}, u32[]{:S(2)}) collective-permute-start(f32[2,800,128]{2,1,0:T(8,128)S(1)} %slice_bitcast_fusion.4), channel_id=1, source_target_pairs={{0,1},{1,0},{2,3},{3,2},{4,5},{5,4},{6,7},{7,6},{8,9},{9,8},{10,11... | collective-permute-start | bytes 2457608 | tf_op jit(solution)/shard_map/ppermute | solution.py:337
  36.2 2.0 %collective-permute-done.5 = f32[2,800,128]{2,1,0:T(8,128)S(1)} collective-permute-done((f32[2,800,128]{2,1,0:T(8,128)S(1)}, f32[2,800,128]{2,1,0:T(8,128)S(1)}, u32[]{:S(2)}, u32[]{:S(2)}) %collective-permute-start.5) | collective-permute-done | bytes 819232 | tf_op jit(solution)/shard_map/ppermute | solution.py:337
  38.1 0.1 fusion.4.after_ref
  38.2 0.3 collective-permute-start.6
  38.6 0.0 copy-start.1
  38.6 3.3 %copy-done.1 = bf16[25,64,2560]{2,1,0:T(8,128)(2,1)S(1)} copy-done((bf16[25,64,2560]{2,1,0:T(8,128)(2,1)S(1)}, bf16[25,64,2560]{2,1,0:T(8,128)(2,1)}, u32[]{:S(2)}) %copy-start.1) | copy-done | bytes 8192024
  41.9 11.4 %main.1 = (f32[4,2,800,128]{3,2,1,0:T(8,128)S(1)}, f32[4,2,800,128]{3,2,1,0:T(8,128)S(1)}) custom-call(s32[5]{0:T(128)S(1)} %stack.24.meta_ref.meta, s32[60]{0:T(128)S(1)} %copy-done.5, s32[60]{0:T(128)S(1)} %copy-done.6, f32[2,20]{1,0:T(2,128)S(1)} %pad_maximum_fusion.5.bounds_ref.bounds, f32[2560,3]{1,0:T(8,128)S(1)} %bitcast.150, ...), custom_call_target="tpu_custom_call" | custom-call | tf_op jit(solution)/shard_map/main/pallas_call | solution.py:246
  53.3 0.0 copy-start.2
  53.3 0.0 copy-start.3
  53.3 0.6 collective-permute-done.6
  53.9 0.1 slice_bitcast_fusion.10
  53.9 1.9 %fusion.1 = (f32[2,800,128]{2,1,0:T(8,128)}, f32[2,800,128]{2,1,0:T(8,128)}) fusion(f32[800,128]{1,0:T(8,128)S(1)} %get-tuple-element.33, pred[2]{0:T(512)(128)(4,1)S(1)} %get-tuple-element.38, pred[2]{0:T(512)(128)(4,1)S(1)} %get-tuple-element.35, f32[4,2,800,128]{3,2,1,0:T(8,128)S(1)} %get-tuple-element.14), kind=kLoop, calls=%fused_computation.3 | loop fusion | flops 819200 | bytes 3687424 | tf_op jit(solution)/shard_map/add | solution.py:345
  55.8 0.0 collective-permute-start.12
  55.8 1.5 %fusion.3 = (f32[2,800,128]{2,1,0:T(8,128)}, f32[2,800,128]{2,1,0:T(8,128)}) fusion(f32[800,128]{1,0:T(8,128)S(1)} %get-tuple-element.34, pred[2]{0:T(512)(128)(4,1)S(1)} %get-tuple-element.36, pred[2]{0:T(512)(128)(4,1)S(1)} %get-tuple-element.37, f32[4,2,800,128]{3,2,1,0:T(8,128)S(1)} %get-tuple-element.13), kind=kLoop, calls=%fused_computation.7 | loop fusion | flops 819200 | bytes 3687424 | tf_op jit(solution)/shard_map/add | solution.py:345
  57.3 0.0 copy-done.2
  57.3 0.5 collective-permute-start.8
  57.8 0.1 collective-permute-start.11
  57.9 0.4 collective-permute-start.7
  58.3 0.2 collective-permute-done.12
  58.5 1.9 %collective-permute-done.8 = f32[2,800,128]{2,1,0:T(8,128)} collective-permute-done((f32[2,800,128]{2,1,0:T(8,128)}, f32[2,800,128]{2,1,0:T(8,128)}, u32[]{:S(2)}, u32[]{:S(2)}) %collective-permute-start.8) | collective-permute-done | bytes 819232 | tf_op jit(solution)/shard_map/ppermute | solution.py:346
  60.4 2.8 %fusion.16 = (f32[800,128]{1,0:T(8,128)S(1)}, f32[800,128]{1,0:T(8,128)S(1)}, f32[800,128]{1,0:T(8,128)S(1)}, f32[800,128]{1,0:T(8,128)}) fusion(f32[2,800,128]{2,1,0:T(8,128)} %collective-permute-done.8, f32[4,2,800,128]{3,2,1,0:T(8,128)} %copy-done.2, pred[]{:T(512)S(6)} %eq.64, f32[2,800,128]{2,1,0:T(8,128)S(1)} %collective-permute-done.6, pred[]{:T(512)S(6)} %eq.68, ...), kind=kLoop, calls=%fused_computation.30 | loop fusion | flops 1228800 | bytes 5734403 | tf_op jit(solution)/shard_map/add | solution.py:348
  63.2 2.5 %collective-permute-start.10 = (f32[800,128]{1,0:T(8,128)S(1)}, f32[800,128]{1,0:T(8,128)S(1)}, u32[]{:S(2)}, u32[]{:S(2)}) collective-permute-start(f32[800,128]{1,0:T(8,128)S(1)} %get-tuple-element.20), channel_id=1, source_target_pairs={{0,2},{1,3},{2,4},{3,5},{4,6},{5,7},{6,0},{7,1},{8,10},{9,11},{10,... | collective-permute-start | bytes 1228808 | tf_op jit(solution)/shard_map/ppermute | solution.py:354
  65.6 1.1 collective-permute-start.13
  66.8 1.2 collective-permute-start.15
  68.0 0.0 collective-permute-done.11
  68.0 2.3 %collective-permute-start.9 = (f32[800,128]{1,0:T(8,128)S(1)}, f32[800,128]{1,0:T(8,128)}, u32[]{:S(2)}, u32[]{:S(2)}) collective-permute-start(f32[800,128]{1,0:T(8,128)S(1)} %get-tuple-element.19), channel_id=1, source_target_pairs={{0,6},{1,7},{2,0},{3,1},{4,2},{5,3},{6,4},{7,5},{8,14},{9,15},{10,... | collective-permute-start | bytes 1228808 | tf_op jit(solution)/shard_map/ppermute | solution.py:356
  70.3 0.0 collective-permute-done.7
  70.3 26.1 %collective-permute-done.10 = f32[800,128]{1,0:T(8,128)S(1)} collective-permute-done((f32[800,128]{1,0:T(8,128)S(1)}, f32[800,128]{1,0:T(8,128)S(1)}, u32[]{:S(2)}, u32[]{:S(2)}) %collective-permute-start.10) | collective-permute-done | bytes 409632 | tf_op jit(solution)/shard_map/ppermute | solution.py:354
  96.5 1.8 %collective-permute-done.13 = f32[800,128]{1,0:T(8,128)S(1)} collective-permute-done((f32[800,128]{1,0:T(8,128)S(1)}, f32[800,128]{1,0:T(8,128)S(1)}, u32[]{:S(2)}, u32[]{:S(2)}) %collective-permute-start.13) | collective-permute-done | bytes 409632 | tf_op jit(solution)/shard_map/ppermute | solution.py:355
  98.2 2.2 %fusion.12 = (f32[800,128]{1,0:T(8,128)}, f32[800,128]{1,0:T(8,128)}) fusion(f32[800,128]{1,0:T(8,128)S(1)} %collective-permute-done.13, f32[2,800,128]{2,1,0:T(8,128)S(1)} %collective-permute-done.11, f32[4,2,800,128]{3,2,1,0:T(8,128)} %copy-done.3, pred[]{:T(512)S(6)} %eq.64, f32[2,800,128]{2,1,0:T(8,128)S(1)} %collective-permute-done.6, ...), kind=kLoop, calls=%fused_computation.22 | loop fusion | flops 819200 | bytes 4096002 | tf_op jit(solution)/shard_map/add | solution.py:360
  100.5 0.4 collective-permute-start.14
  100.9 3.1 %collective-permute-start.16 = (f32[800,128]{1,0:T(8,128)}, f32[800,128]{1,0:T(8,128)}, u32[]{:S(2)}, u32[]{:S(2)}) collective-permute-start(f32[800,128]{1,0:T(8,128)} %get-tuple-element.16), channel_id=1, source_target_pairs={{0,6},{1,7},{2,0},{3,1},{4,2},{5,3},{6,4},{7,5},{8,14},{9,15},{10,... | collective-permute-start | bytes 1228808 | tf_op jit(solution)/shard_map/ppermute | solution.py:362
  104.1 7.5 %collective-permute-done.15 = f32[800,128]{1,0:T(8,128)S(1)} collective-permute-done((f32[800,128]{1,0:T(8,128)}, f32[800,128]{1,0:T(8,128)S(1)}, u32[]{:S(2)}, u32[]{:S(2)}) %collective-permute-start.15) | collective-permute-done | bytes 409632 | tf_op jit(solution)/shard_map/ppermute | solution.py:357
  111.6 1.5 %collective-permute-done.9 = f32[800,128]{1,0:T(8,128)} collective-permute-done((f32[800,128]{1,0:T(8,128)S(1)}, f32[800,128]{1,0:T(8,128)}, u32[]{:S(2)}, u32[]{:S(2)}) %collective-permute-start.9) | collective-permute-done | bytes 409632 | tf_op jit(solution)/shard_map/ppermute | solution.py:356
  113.1 7.4 %collective-permute-done.14 = f32[800,128]{1,0:T(8,128)} collective-permute-done((f32[800,128]{1,0:T(8,128)}, f32[800,128]{1,0:T(8,128)}, u32[]{:S(2)}, u32[]{:S(2)}) %collective-permute-start.14) | collective-permute-done | bytes 409632 | tf_op jit(solution)/shard_map/ppermute | solution.py:361
  120.5 1.4 %collective-permute-done.16 = f32[800,128]{1,0:T(8,128)} collective-permute-done((f32[800,128]{1,0:T(8,128)}, f32[800,128]{1,0:T(8,128)}, u32[]{:S(2)}, u32[]{:S(2)}) %collective-permute-start.16) | collective-permute-done | bytes 409632 | tf_op jit(solution)/shard_map/ppermute | solution.py:362
  121.9 1.7 %fusion.20 = (bf16[800,128]{1,0:T(8,128)(2,1)S(1)}, bf16[800,128]{1,0:T(8,128)(2,1)S(1)}) fusion(f32[800,128]{1,0:T(8,128)} %collective-permute-done.14, f32[800,128]{1,0:T(8,128)} %collective-permute-done.9, f32[2,800,128]{2,1,0:T(8,128)S(1)} %collective-permute-done.7, f32[4,2,800,128]{3,2,1,0:T(8,128)} %copy-done.2, pred[]{:T(512)S(6)} %eq.60, ...), kind=kLoop, calls=%fused_computation.35 | loop fusion | flops 1228800 | bytes 4505601 | tf_op jit(solution)/shard_map/convert_element_type | solution.py:365
  123.6 0.8 pad_maximum_fusion
  (11 shorter events, 0.1 us)
Async XLA Ops:
  2.2 13.5 %collective-permute-start = (f32[5,128]{1,0:T(8,128)S(1)}, f32[5,128]{1,0:T(8,128)S(1)}, u32[]{:S(2)}, u32[]{:S(2)}) collective-permute-start(f32[5,128]{1,0:T(8,128)S(1)} %pad_maximum_fusion.4), channel_id=1, source_target_pairs={{0,8},{8,16},{16,24},{24,32},{32,40},{40,48},{48,56},{56,64},{64,7... | collective-permute-start | bytes 7688 | tf_op jit(solution)/shard_map/ppermute | solution.py:310
  4.3 11.3 %collective-permute-start.1 = (f32[5,128]{1,0:T(8,128)S(1)}, f32[5,128]{1,0:T(8,128)S(1)}, u32[]{:S(2)}, u32[]{:S(2)}) collective-permute-start(f32[5,128]{1,0:T(8,128)S(1)} %pad_maximum_fusion.4), channel_id=1, source_target_pairs={{8,0},{16,8},{24,16},{32,24},{40,32},{48,40},{56,48},{64,56},{72,6... | collective-permute-start | bytes 7688 | tf_op jit(solution)/shard_map/ppermute | solution.py:311
  12.3 16.9 %copy-start.4 = (f32[3,128]{1,0:T(4,128)S(1)}, f32[3,128]{1,0:T(4,128)}, u32[]{:S(2)}) copy-start(f32[3,128]{1,0:T(4,128)} %after_ref.1) | copy-start | bytes 4612
  12.3 16.9 %copy-start.5 = (s32[60]{0:T(128)S(1)}, s32[60]{0:T(128)}, u32[]{:S(2)}) copy-start(s32[60]{0:T(128)} %tile_ref.3) | copy-start | bytes 724
  12.3 16.9 %copy-start.6 = (s32[60]{0:T(128)S(1)}, s32[60]{0:T(128)}, u32[]{:S(2)}) copy-start(s32[60]{0:T(128)} %block_ref.3) | copy-start | bytes 724
  15.6 16.2 %copy-start = (bf16[25,64,2560]{2,1,0:T(8,128)(2,1)}, bf16[25,64,2560]{2,1,0:T(8,128)(2,1)S(1)}, u32[]{:S(2)}) copy-start(bf16[25,64,2560]{2,1,0:T(8,128)(2,1)S(1)} %get-tuple-element.12.cot_ref) | copy-start | bytes 24576004
  15.7 3.3 %collective-permute-start.2 = (f32[1,15,128]{2,1,0:T(8,128)S(1)}, f32[1,15,128]{2,1,0:T(8,128)S(1)}, u32[]{:S(2)}, u32[]{:S(2)}) collective-permute-start(f32[1,15,128]{2,1,0:T(8,128)S(1)} %fusion.21), channel_id=1, source_target_pairs={{0,1},{1,0},{2,3},{3,2},{4,5},{5,4},{6,7},{7,6},{8,9},{9,8},{10,11... | collective-permute-start | bytes 23048 | tf_op jit(solution)/shard_map/ppermute | solution.py:321
  19.0 3.5 %collective-permute-start.3 = (f32[2,15,128]{2,1,0:T(8,128)S(1)}, f32[2,15,128]{2,1,0:T(8,128)S(1)}, u32[]{:S(2)}, u32[]{:S(2)}) collective-permute-start(f32[2,15,128]{2,1,0:T(8,128)S(1)} %pad_maximum_fusion.3), channel_id=1, source_target_pairs={{0,2},{1,3},{2,0},{3,1},{4,6},{5,7},{6,4},{7,5},{8,10},{9,11},{10,... | collective-permute-start | bytes 46088 | tf_op jit(solution)/shard_map/ppermute | solution.py:321
  22.5 6.7 %collective-permute-start.4 = (f32[4,15,128]{2,1,0:T(8,128)S(1)}, f32[4,15,128]{2,1,0:T(8,128)S(1)}, u32[]{:S(2)}, u32[]{:S(2)}) collective-permute-start(f32[4,15,128]{2,1,0:T(8,128)S(1)} %pad_maximum_fusion.2), channel_id=1, source_target_pairs={{0,4},{1,5},{2,6},{3,7},{4,0},{5,1},{6,2},{7,3},{8,12},{9,13},{10,... | collective-permute-start | bytes 92168 | tf_op jit(solution)/shard_map/ppermute | solution.py:321
  31.9 6.2 %collective-permute-start.5 = (f32[2,800,128]{2,1,0:T(8,128)S(1)}, f32[2,800,128]{2,1,0:T(8,128)S(1)}, u32[]{:S(2)}, u32[]{:S(2)}) collective-permute-start(f32[2,800,128]{2,1,0:T(8,128)S(1)} %slice_bitcast_fusion.4), channel_id=1, source_target_pairs={{0,1},{1,0},{2,3},{3,2},{4,5},{5,4},{6,7},{7,6},{8,9},{9,8},{10,11... | collective-permute-start | bytes 2457608 | tf_op jit(solution)/shard_map/ppermute | solution.py:337
  38.2 15.7 %collective-permute-start.6 = (f32[2,800,128]{2,1,0:T(8,128)S(1)}, f32[2,800,128]{2,1,0:T(8,128)S(1)}, u32[]{:S(2)}, u32[]{:S(2)}) collective-permute-start(f32[2,800,128]{2,1,0:T(8,128)S(1)} %fusion.4.after_ref), channel_id=1, source_target_pairs={{0,248},{1,9},{2,250},{3,11},{4,252},{5,13},{6,254},{7,15},{8,0},{... | collective-permute-start | bytes 2457608 | tf_op jit(solution)/shard_map/ppermute | solution.py:338
  38.6 3.3 %copy-start.1 = (bf16[25,64,2560]{2,1,0:T(8,128)(2,1)S(1)}, bf16[25,64,2560]{2,1,0:T(8,128)(2,1)}, u32[]{:S(2)}) copy-start(bf16[25,64,2560]{2,1,0:T(8,128)(2,1)} %copy-done) | copy-start | bytes 24576004
  53.3 4.0 %copy-start.2 = (f32[4,2,800,128]{3,2,1,0:T(8,128)}, f32[4,2,800,128]{3,2,1,0:T(8,128)S(1)}, u32[]{:S(2)}) copy-start(f32[4,2,800,128]{3,2,1,0:T(8,128)S(1)} %get-tuple-element.13) | copy-start | bytes 9830404
  53.3 4.0 %copy-start.3 = (f32[4,2,800,128]{3,2,1,0:T(8,128)}, f32[4,2,800,128]{3,2,1,0:T(8,128)S(1)}, u32[]{:S(2)}) copy-start(f32[4,2,800,128]{3,2,1,0:T(8,128)S(1)} %get-tuple-element.14) | copy-start | bytes 9830404
  55.8 2.7 %collective-permute-start.12 = (f32[2,800,128]{2,1,0:T(8,128)}, f32[2,800,128]{2,1,0:T(8,128)}, u32[]{:S(2)}, u32[]{:S(2)}) collective-permute-start(f32[2,800,128]{2,1,0:T(8,128)} %get-tuple-element.24), channel_id=1, source_target_pairs={{0,1},{1,0},{2,3},{3,2},{4,5},{5,4},{6,7},{7,6},{8,9},{9,8},{10,11... | collective-permute-start | bytes 2457608 | tf_op jit(solution)/shard_map/ppermute | solution.py:346
  57.3 3.1 %collective-permute-start.8 = (f32[2,800,128]{2,1,0:T(8,128)}, f32[2,800,128]{2,1,0:T(8,128)}, u32[]{:S(2)}, u32[]{:S(2)}) collective-permute-start(f32[2,800,128]{2,1,0:T(8,128)} %get-tuple-element.26), channel_id=1, source_target_pairs={{0,1},{1,0},{2,3},{3,2},{4,5},{5,4},{6,7},{7,6},{8,9},{9,8},{10,11... | collective-permute-start | bytes 2457608 | tf_op jit(solution)/shard_map/ppermute | solution.py:346
  57.8 10.2 %collective-permute-start.11 = (f32[2,800,128]{2,1,0:T(8,128)}, f32[2,800,128]{2,1,0:T(8,128)S(1)}, u32[]{:S(2)}, u32[]{:S(2)}) collective-permute-start(f32[2,800,128]{2,1,0:T(8,128)} %get-tuple-element.23), channel_id=1, source_target_pairs={{0,1},{1,0},{2,3},{3,2},{4,5},{5,4},{6,7},{7,6},{8,9},{9,8},{10,11... | collective-permute-start | bytes 2457608 | tf_op jit(solution)/shard_map/ppermute | solution.py:346
  57.9 12.4 %collective-permute-start.7 = (f32[2,800,128]{2,1,0:T(8,128)}, f32[2,800,128]{2,1,0:T(8,128)S(1)}, u32[]{:S(2)}, u32[]{:S(2)}) collective-permute-start(f32[2,800,128]{2,1,0:T(8,128)} %get-tuple-element.25), channel_id=1, source_target_pairs={{0,1},{1,0},{2,3},{3,2},{4,5},{5,4},{6,7},{7,6},{8,9},{9,8},{10,11... | collective-permute-start | bytes 2457608 | tf_op jit(solution)/shard_map/ppermute | solution.py:346
  63.2 33.3 %collective-permute-start.10 = (f32[800,128]{1,0:T(8,128)S(1)}, f32[800,128]{1,0:T(8,128)S(1)}, u32[]{:S(2)}, u32[]{:S(2)}) collective-permute-start(f32[800,128]{1,0:T(8,128)S(1)} %get-tuple-element.20), channel_id=1, source_target_pairs={{0,2},{1,3},{2,4},{3,5},{4,6},{5,7},{6,0},{7,1},{8,10},{9,11},{10,... | collective-permute-start | bytes 1228808 | tf_op jit(solution)/shard_map/ppermute | solution.py:354
  65.6 32.6 %collective-permute-start.13 = (f32[800,128]{1,0:T(8,128)S(1)}, f32[800,128]{1,0:T(8,128)S(1)}, u32[]{:S(2)}, u32[]{:S(2)}) collective-permute-start(f32[800,128]{1,0:T(8,128)S(1)} %get-tuple-element.29), channel_id=1, source_target_pairs={{0,6},{1,7},{2,0},{3,1},{4,2},{5,3},{6,4},{7,5},{8,14},{9,15},{10,... | collective-permute-start | bytes 1228808 | tf_op jit(solution)/shard_map/ppermute | solution.py:355
  66.8 44.8 %collective-permute-start.15 = (f32[800,128]{1,0:T(8,128)}, f32[800,128]{1,0:T(8,128)S(1)}, u32[]{:S(2)}, u32[]{:S(2)}) collective-permute-start(f32[800,128]{1,0:T(8,128)} %get-tuple-element.30), channel_id=1, source_target_pairs={{0,2},{1,3},{2,4},{3,5},{4,6},{5,7},{6,0},{7,1},{8,10},{9,11},{10,... | collective-permute-start | bytes 1228808 | tf_op jit(solution)/shard_map/ppermute | solution.py:357
  68.0 45.1 %collective-permute-start.9 = (f32[800,128]{1,0:T(8,128)S(1)}, f32[800,128]{1,0:T(8,128)}, u32[]{:S(2)}, u32[]{:S(2)}) collective-permute-start(f32[800,128]{1,0:T(8,128)S(1)} %get-tuple-element.19), channel_id=1, source_target_pairs={{0,6},{1,7},{2,0},{3,1},{4,2},{5,3},{6,4},{7,5},{8,14},{9,15},{10,... | collective-permute-start | bytes 1228808 | tf_op jit(solution)/shard_map/ppermute | solution.py:356
  100.5 20.0 %collective-permute-start.14 = (f32[800,128]{1,0:T(8,128)}, f32[800,128]{1,0:T(8,128)}, u32[]{:S(2)}, u32[]{:S(2)}) collective-permute-start(f32[800,128]{1,0:T(8,128)} %get-tuple-element.15), channel_id=1, source_target_pairs={{0,2},{1,3},{2,4},{3,5},{4,6},{5,7},{6,0},{7,1},{8,10},{9,11},{10,... | collective-permute-start | bytes 1228808 | tf_op jit(solution)/shard_map/ppermute | solution.py:361
  100.9 21.0 %collective-permute-start.16 = (f32[800,128]{1,0:T(8,128)}, f32[800,128]{1,0:T(8,128)}, u32[]{:S(2)}, u32[]{:S(2)}) collective-permute-start(f32[800,128]{1,0:T(8,128)} %get-tuple-element.16), channel_id=1, source_target_pairs={{0,6},{1,7},{2,0},{3,1},{4,2},{5,3},{6,4},{7,5},{8,14},{9,15},{10,... | collective-permute-start | bytes 1228808 | tf_op jit(solution)/shard_map/ppermute | solution.py:362
